TPU v7x, 512 devices: a whole 4x4x16 slice. The times are simulated.
512 devices in a mesh: ctx: 64 (over y, z_lo, core), tp: 8 (over z_hi, x).
Axes of the slice: x: 4, y: 4, z: 16 (z_hi: 2, z_lo: 8; z = z_hi * 8 + z_lo), core: 2. Of those that a mesh axis runs over, the one named last changes fastest.
Arguments:
- qkv_values: bfloat16 [16384, 3, 8192], P('ctx', None, 'tp'), may hold values from -6 to 6
- short_taps: float32 [7, 3, 8192], P(None, None, 'tp'), may hold values from -2 to 2
- medium_taps: float32 [128, 8192], P(None, 'tp'), may hold values from -0.5 to 0.5
- skip_gain: float32 [8192], P('tp'), may hold values from -4 to 4
- out_weight: bfloat16 [8192, 4096], P('tp', 'ctx'), may hold values from -0.0625 to 0.0625
Outputs:
- block_out: bfloat16 [16384, 4096], P('ctx', 'tp')
All inputs are finite; a program needn't handle non-finite values.
Results may differ from a plain program's by a relative error of at most 0.015.
Values may be sent and summed in bfloat16 or wider, within the bound.
A program may use at most 64 MiB of HBM per device.

v0:
```python
import jax
import jax.numpy as jnp
from jax import lax
from jax.sharding import PartitionSpec as P


def shifted(value, axis, steps):
    count = lax.axis_size(axis)
    first, last = (max(0, -steps), min(count, count - steps))
    return lax.ppermute(value, axis, [(source, source + steps) for source in range(first, last)])


def causal_taps(extended, tap_table, length):
    tap_count = tap_table.shape[0]
    first_row = extended.shape[0] - length
    summed = jnp.zeros((length,) + extended.shape[1:], jnp.float32)
    for offset in range(tap_count):
        window = lax.slice_in_dim(extended, first_row - offset, first_row - offset + length, axis=0)
        summed = summed + tap_table[offset] * window.astype(jnp.float32)
    return summed


def on_device(qkv_values, short_taps, medium_taps, skip_gain, out_weight):
    tokens_here = qkv_values.shape[0]
    short_reach = short_taps.shape[0] - 1
    medium_reach = medium_taps.shape[0] - 1
    before = shifted(qkv_values[tokens_here - short_reach :], "ctx", 1)
    extended = jnp.concatenate([before, qkv_values], axis=0)
    shortened = causal_taps(extended, short_taps, tokens_here)
    queries = shortened[:, 0]
    product = shortened[:, 1] * shortened[:, 2]
    earlier = shifted(product[tokens_here - medium_reach :], "ctx", 1)
    product_ext = jnp.concatenate([earlier, product], axis=0)
    carried = causal_taps(product_ext, medium_taps, tokens_here)
    gated_out = (queries * (carried + skip_gain * product)).astype(jnp.bfloat16)
    partials = jnp.dot(
        gated_out,
        lax.all_gather(out_weight, "ctx", axis=1, tiled=True),
        preferred_element_type=jnp.float32,
    )
    summed = lax.psum_scatter(partials.astype(jnp.bfloat16), "tp", scatter_dimension=1, tiled=True)
    return summed


def solution(mesh):
    return jax.shard_map(
        on_device,
        mesh=mesh,
        in_specs=(
            P("ctx", None, "tp"),
            P(None, None, "tp"),
            P(None, "tp"),
            P("tp"),
            P("tp", "ctx"),
        ),
        out_specs=P("ctx", "tp"),
        check_vma=False,
    )
```

profile of v0, /device:TPU:8, one launch (start us, length us, event | category | flops | bytes accessed | tf_op | source)
XLA Modules:
  0.0 304.1 jit_solution(7082663197515116327)
XLA Ops:
  6.5 0.0 all-gather.2.cloned.1.call-start
  6.5 0.7 all-gather.2.cloned.1.call-update
  7.3 0.0 reduce-scatter.2.cloned.1.call-start
  7.3 0.8 slice.824
  8.1 1.9 collective-permute-start
  10.0 1.3 fusion.397
  11.4 1.1 fusion.396
  12.6 1.4 fusion.391
  14.0 1.4 fusion.390
  15.4 1.4 fusion.395
  16.8 5.6 %collective-permute-done = bf16[6,3,1024]{2,0,1:T(8,128)(2,1)S(1)} collective-permute-done((bf16[6,3,1024]{2,0,1:T(8,128)(2,1)S(1)}, bf16[6,3,1024]{2,0,1:T(8,128)(2,1)S(1)}, u32[]{:S(2)}, u32[]{:S(2)}) %collective-permute-start) | collective-permute-done | bytes 36896 | tf_op jit(solution)/shard_map/ppermute | solution.py:10
  22.4 7.1 %multiply_add_fusion = f32[256,3,1024]{2,0,1:T(8,128)S(1)} fusion(bf16[256,3,1024]{2,0,1:T(8,128)(2,1)} %param.5, bf16[6,3,1024]{2,0,1:T(8,128)(2,1)S(1)} %collective-permute-done, f32[3,1024]{1,0:T(4,128)S(1)} %get-tuple-element.142, f32[3,1024]{1,0:T(4,128)S(1)} %get-tuple-element.143, f32[3,1024]{1,0:T(4,128)S(1)} %get-tuple-element.144, ...), kind=kLoop, calls=%fused_computation.258 | loop fusion | flops 29884416 | bytes 4841472 | tf_op jit(solution)/shard_map/add | solution.py:19
  29.5 0.0 copy-start
  29.5 0.3 broadcast_multiply_fusion
  29.8 1.9 collective-permute-start.1
  31.8 1.3 fusion.394
  33.1 1.4 fusion.393
  34.5 1.4 fusion.392
  35.9 16.9 %collective-permute-done.1 = f32[127,1024]{1,0:T(8,128)S(1)} collective-permute-done((f32[127,1024]{1,0:T(8,128)S(1)}, f32[127,1024]{1,0:T(8,128)S(1)}, u32[]{:S(2)}, u32[]{:S(2)}) %collective-permute-start.1) | collective-permute-done | bytes 520224 | tf_op jit(solution)/shard_map/ppermute | solution.py:10
  52.8 0.0 copy-done
  52.8 26.8 %fusion.487 = bf16[256,1024]{1,0:T(8,128)(2,1)S(1)} fusion(f32[256,1024]{1,0:T(8,128)S(1)} %bitcast.158, f32[127,1024]{1,0:T(8,128)S(1)} %collective-permute-done.1, f32[256,3,1024]{2,0,1:T(8,128)S(1)} %multiply_add_fusion, f32[1024]{0:T(1024)S(1)} %copy-done, f32[1024]{0:T(1024)S(1)} %bitcast.171, f32[1024]{0:T(1024)S(1)} %bitcast.172, ...), kind=kLoop, calls=%fused_computation.274.clone.clone.1 | loop fusion | flops 100925440 | bytes 4714496 | tf_op jit(solution)/shard_map/dot_general | solution.py:36
  79.6 62.6 %all-gather.2.cloned.1.call-done = bf16[1024,4096]{0,1:T(8,128)(2,1)} async-done(((bf16[1024,64]{0,1:T(8,128)(2,1)}), bf16[1024,4096]{0,1:T(8,128)(2,1)}) %all-gather.2.cloned.1.call-update) | async-done | bytes 8388624 | tf_op jit(solution)/shard_map/all_gather | solution.py:38
  142.3 7.1 %convolution_convert_fusion = bf16[256,4096]{1,0:T(8,128)(2,1)} fusion(bf16[1024,4096]{0,1:T(8,128)(2,1)} %all-gather.2.cloned.1.call-done, bf16[256,1024]{1,0:T(8,128)(2,1)S(1)} %fusion.487), kind=kOutput, calls=%fused_computation.252 | convolution fusion | flops 2148532224 | bytes 11010048 | tf_op jit(solution)/shard_map/dot_general | solution.py:36
  149.4 0.0 reduce-scatter.2.cloned.1.call-update
  149.4 147.8 %reduce-scatter.2.cloned.1.call-done = bf16[256,512]{1,0:T(8,128)(2,1)} async-done(((bf16[256,4096]{1,0:T(8,128)(2,1)}), bf16[256,512]{1,0:T(8,128)(2,1)}) %reduce-scatter.2.cloned.1.call-update) | async-done | bytes 262160 | tf_op jit(solution)/shard_map/reduce_scatter | solution.py:41
  (5 shorter events, 0.1 us)
Async XLA Ops:
  6.5 135.7 %all-gather.2.cloned.1.call-start = ((), (), s32[]{:S(2)}) async-start(), calls=%async_computation.1 | async-start | bytes 8519680 | tf_op jit(solution)/shard_map/all_gather | solution.py:38
  7.3 290.0 %reduce-scatter.2.cloned.1.call-start = ((), (), s32[]{:S(2)}) async-start(), calls=%async_computation.2 | async-start | bytes 2359296 | tf_op jit(solution)/shard_map/reduce_scatter | solution.py:41
  8.1 14.3 %collective-permute-start = (bf16[6,3,1024]{2,0,1:T(8,128)(2,1)S(1)}, bf16[6,3,1024]{2,0,1:T(8,128)(2,1)S(1)}, u32[]{:S(2)}, u32[]{:S(2)}) collective-permute-start(bf16[6,3,1024]{2,0,1:T(8,128)(2,1)S(1)} %slice.824), channel_id=1, source_target_pairs={{0,8},{8,16},{16,24},{24,32},{32,40},{40,48},{48,56},{56,64},{64,7... | collective-permute-start | bytes 110600 | tf_op jit(solution)/shard_map/ppermute | solution.py:10
  29.5 23.3 %copy-start = (f32[1024]{0:T(1024)S(1)}, f32[1024]{0:T(1024)}, u32[]{:S(2)}) copy-start(f32[1024]{0:T(1024)} %param.8) | copy-start | bytes 12292
  29.8 22.9 %collective-permute-start.1 = (f32[127,1024]{1,0:T(8,128)S(1)}, f32[127,1024]{1,0:T(8,128)S(1)}, u32[]{:S(2)}, u32[]{:S(2)}) collective-permute-start(f32[127,1024]{1,0:T(8,128)S(1)} %slice_bitcast_fusion.1), channel_id=1, source_target_pairs={{0,8},{8,16},{16,24},{24,32},{32,40},{40,48},{48,56},{56,64},{64,7... | collective-permute-start | bytes 1560584 | tf_op jit(solution)/shard_map/ppermute | solution.py:10
Sparse Core Ops, SparseCore 0:
  9.5 132.7 all-gather.1
  149.5 147.6 reduce-scatter.1
where the time goes:
time: 305 us; the launch traced here: 304 us
  waiting for transfers between devices  234 us (77%)
  other arithmetic  34.2 us (11%)
  between operations  13.5 us (4%)
  local copies, waits for them, and re-layouts  11.6 us (4%)
  matrix products  7.14 us (2%)
  starting transfers between devices  3.88 us (1%)
    reduce_scatter x1, waiting for transfers between devices, on_device(): lax.psum_scatter(partials.astype(jnp.bfloat16), 'tp', scatter_dimension=1...  148 us
    all_gather x1, waiting for transfers between devices, on_device(): lax.all_gather(out_weight, 'ctx', axis=1, tiled=True)  62.6 us
    dot_general x1, other arithmetic, on_device(): jnp.dot(gated_out, lax.all_gather(out_weight, 'ctx', axis=1, tiled=True),...  26.8 us
    ppermute x2, waiting for transfers between devices, shifted(): lax.ppermute(value, axis, [(source, source + steps) for source in range(f...  22.5 us
    slice x8, local copies, waits for them, and re-layouts, causal_taps(): summed = summed + tap_table[offset] * window.astype(jnp.float32)  10.7 us
    dot_general x1, matrix products, on_device(): jnp.dot(gated_out, lax.all_gather(out_weight, 'ctx', axis=1, tiled=True),...  7.14 us
    add x1, other arithmetic, causal_taps(): summed = summed + tap_table[offset] * window.astype(jnp.float32)  7.09 us
  transfers between devices with their start and end apart: 4, of which 4 were waited for; matrix products, arithmetic and copies ran while one was open for 15% of the time, Pallas kernels for 0%

commit v1 on v0

--- a/solution.py
+++ b/solution.py
@@ -35,7 +35,9 @@
     gated_out = (queries * (carried + skip_gain * product)).astype(jnp.bfloat16)
     partials = jnp.dot(
         gated_out,
-        lax.all_gather(out_weight, "ctx", axis=1, tiled=True),
+        jnp.concatenate(
+            lax.all_to_all(jnp.stack([out_weight] * lax.axis_size("ctx")), "ctx", 0, 0), axis=1
+        ),
         preferred_element_type=jnp.float32,
     )
     summed = lax.psum_scatter(partials.astype(jnp.bfloat16), "tp", scatter_dimension=1, tiled=True)

time: 305 us -> 590 us (1.93)
  the two profiles are of different devices: /device:TPU:8 before, /device:TPU:16 now
where the time goes in v1:
time: 590 us; the launch traced here: 589 us
  waiting for transfers between devices  512 us (87%)
  other arithmetic  30 us (5%)
  starting transfers between devices  20.5 us (3%)
  between operations  13.6 us (2%)
  matrix products  7.14 us (1%)
    reduce_scatter x1, waiting for transfers between devices, on_device(): lax.psum_scatter(partials.astype(jnp.bfloat16), 'tp', scatter_dimension=1...  182 us
    ppermute x2, waiting for transfers between devices, shifted(): lax.ppermute(value, axis, [(source, source + steps) for source in range(f...  181 us
    all_to_all x1, waiting for transfers between devices, on_device(): lax.all_to_all(jnp.stack([out_weight] * lax.axis_size('ctx')), 'ctx', 0, 0)  149 us
    dot_general x1, other arithmetic, on_device(): jnp.dot(gated_out, jnp.concatenate(lax.all_to_all(jnp.stack([out_weight]...  26.9 us
    all_to_all x1, starting transfers between devices, on_device(): lax.all_to_all(jnp.stack([out_weight] * lax.axis_size('ctx')), 'ctx', 0, 0)  16.5 us
  transfers between devices with their start and end apart: 4, of which 4 were waited for; matrix products, arithmetic and copies ran while one was open for 5% of the time, Pallas kernels for 0%

profile of v1, /device:TPU:16, one launch (start us, length us, event | category | flops | bytes accessed | tf_op | source)
XLA Modules:
  0.0 589.4 jit_solution(10323329202872752781)
XLA Ops:
  6.5 5.2 stack.2
  11.7 0.0 copy-start
  11.7 0.0 copy-start.2
  11.7 0.0 copy-start.1
  11.7 16.5 %all-to-all-start = ((bf16[64,1024,64]{1,2,0:T(8,128)(2,1)}), bf16[64,1024,64]{1,2,0:T(8,128)(2,1)}, u32[]{:S(2)}, u32[]{:S(2)}) async-start(bf16[64,1024,64]{1,2,0:T(8,128)(2,1)} %stack.2), calls=%async_computation | async-start | bytes 16777216 | tf_op jit(solution)/shard_map/all_to_all | solution.py:39
  28.2 0.0 reduce-scatter.2.cloned.1.call-start
  28.3 0.0 copy-done
  28.3 2.1 collective-permute-start
  30.4 0.0 copy-done.2
  30.4 0.1 fusion.397
  30.5 0.0 copy-done.1
  30.5 0.1 fusion.390
  30.6 0.1 fusion.391
  30.7 0.1 fusion.392
  30.8 164.9 %collective-permute-done = bf16[6,3,1024]{2,0,1:T(8,128)(2,1)S(1)} collective-permute-done((bf16[6,3,1024]{2,0,1:T(8,128)(2,1)S(1)}, bf16[6,3,1024]{2,0,1:T(8,128)(2,1)S(1)}, u32[]{:S(2)}, u32[]{:S(2)}) %collective-permute-start) | collective-permute-done | bytes 36896 | tf_op jit(solution)/shard_map/ppermute | solution.py:10
  195.7 2.9 multiply_add_fusion
  198.5 0.0 copy-start.3
  198.6 0.3 broadcast_multiply_fusion
  198.9 0.1 slice_bitcast_fusion.1
  198.9 1.9 collective-permute-start.1
  200.9 0.1 fusion.393
  200.9 0.1 fusion.394
  201.0 0.1 fusion.395
  201.1 16.1 %collective-permute-done.1 = f32[127,1024]{1,0:T(8,128)S(1)} collective-permute-done((f32[127,1024]{1,0:T(8,128)S(1)}, f32[127,1024]{1,0:T(8,128)S(1)}, u32[]{:S(2)}, u32[]{:S(2)}) %collective-permute-start.1) | collective-permute-done | bytes 520224 | tf_op jit(solution)/shard_map/ppermute | solution.py:10
  217.2 0.0 copy-done.3
  217.2 26.9 %fusion.487 = bf16[256,1024]{1,0:T(8,128)(2,1)S(1)} fusion(f32[256,1024]{1,0:T(8,128)S(1)} %bitcast.161, f32[127,1024]{1,0:T(8,128)S(1)} %collective-permute-done.1, f32[256,3,1024]{2,0,1:T(8,128)S(1)} %multiply_add_fusion, f32[1024]{0:T(1024)S(1)} %copy-done.3, f32[1024]{0:T(1024)S(1)} %bitcast.174, f32[1024]{0:T(1024)S(1)} %bitcast.175, ...), kind=kLoop, calls=%fused_computation.274.clone.clone.1 | loop fusion | flops 100925440 | bytes 4714496 | tf_op jit(solution)/shard_map/dot_general | solution.py:36
  244.0 149.4 %all-to-all-done = bf16[64,1024,64]{1,2,0:T(8,128)(2,1)} async-done(((bf16[64,1024,64]{1,2,0:T(8,128)(2,1)}), bf16[64,1024,64]{1,2,0:T(8,128)(2,1)}, u32[]{:S(2)}, u32[]{:S(2)}) %all-to-all-start) | async-done | bytes 8388640 | tf_op jit(solution)/shard_map/all_to_all | solution.py:39
  393.4 7.1 %convolution_convert_fusion = bf16[256,4096]{1,0:T(8,128)(2,1)} fusion(bf16[1024,4096]{0,1:T(8,128)(2,1)} %bitcast.132, bf16[256,1024]{1,0:T(8,128)(2,1)S(1)} %fusion.487), kind=kOutput, calls=%fused_computation.252 | convolution fusion | flops 2148532224 | bytes 11010048 | tf_op jit(solution)/shard_map/dot_general | solution.py:36
  400.5 0.0 reduce-scatter.2.cloned.1.call-update
  400.6 182.0 %reduce-scatter.2.cloned.1.call-done = bf16[256,512]{1,0:T(8,128)(2,1)} async-done(((bf16[256,4096]{1,0:T(8,128)(2,1)}), bf16[256,512]{1,0:T(8,128)(2,1)}) %reduce-scatter.2.cloned.1.call-update) | async-done | bytes 262160 | tf_op jit(solution)/shard_map/reduce_scatter | solution.py:43
  (6 shorter events, 0.1 us)
Async XLA Ops:
  11.7 16.5 %copy-start = (bf16[256,3,1024]{2,0,1:T(8,128)(2,1)S(1)}, bf16[256,3,1024]{2,0,1:T(8,128)(2,1)}, u32[]{:S(2)}) copy-start(bf16[256,3,1024]{2,0,1:T(8,128)(2,1)} %param.5) | copy-start | bytes 4718596
  11.7 18.6 %copy-start.2 = (f32[7,3,1024]{2,0,1:T(8,128)S(1)}, f32[7,3,1024]{2,0,1:T(8,128)}, u32[]{:S(2)}) copy-start(f32[7,3,1024]{2,0,1:T(8,128)} %param.6) | copy-start | bytes 258052
  11.7 18.7 %copy-start.1 = (f32[128,1024]{1,0:T(8,128)S(1)}, f32[128,1024]{1,0:T(8,128)}, u32[]{:S(2)}) copy-start(f32[128,1024]{1,0:T(8,128)} %param.7) | copy-start | bytes 1572868
  11.7 381.6 %all-to-all-start = ((bf16[64,1024,64]{1,2,0:T(8,128)(2,1)}), bf16[64,1024,64]{1,2,0:T(8,128)(2,1)}, u32[]{:S(2)}, u32[]{:S(2)}) async-start(bf16[64,1024,64]{1,2,0:T(8,128)(2,1)} %stack.2), calls=%async_computation | async-start | bytes 16777216 | tf_op jit(solution)/shard_map/all_to_all | solution.py:39
  28.2 554.4 %reduce-scatter.2.cloned.1.call-start = ((), (), s32[]{:S(2)}) async-start(), calls=%async_computation.2 | async-start | bytes 2359296 | tf_op jit(solution)/shard_map/reduce_scatter | solution.py:43
  28.3 167.4 %collective-permute-start = (bf16[6,3,1024]{2,0,1:T(8,128)(2,1)S(1)}, bf16[6,3,1024]{2,0,1:T(8,128)(2,1)S(1)}, u32[]{:S(2)}, u32[]{:S(2)}) collective-permute-start(bf16[6,3,1024]{2,0,1:T(8,128)(2,1)S(1)} %slice.824), channel_id=1, source_target_pairs={{0,8},{8,16},{16,24},{24,32},{32,40},{40,48},{48,56},{56,64},{64,7... | collective-permute-start | bytes 110600 | tf_op jit(solution)/shard_map/ppermute | solution.py:10
  198.5 18.6 %copy-start.3 = (f32[1024]{0:T(1024)S(1)}, f32[1024]{0:T(1024)}, u32[]{:S(2)}) copy-start(f32[1024]{0:T(1024)} %param.8) | copy-start | bytes 12292
  198.9 18.2 %collective-permute-start.1 = (f32[127,1024]{1,0:T(8,128)S(1)}, f32[127,1024]{1,0:T(8,128)S(1)}, u32[]{:S(2)}, u32[]{:S(2)}) collective-permute-start(f32[127,1024]{1,0:T(8,128)S(1)} %slice_bitcast_fusion.1), channel_id=1, source_target_pairs={{0,8},{8,16},{16,24},{24,32},{32,40},{40,48},{48,56},{56,64},{64,7... | collective-permute-start | bytes 1560584 | tf_op jit(solution)/shard_map/ppermute | solution.py:10
Sparse Core Ops, SparseCore 0:
  400.7 181.8 reduce-scatter.1
